TPU v7x, 256 devices: a whole 4x4x8 slice. The times are simulated.
256 devices in a mesh: expert: 32 (over x, z), mp: 8 (over y, core).
Axes of the slice: x: 4, y: 4, z: 8, core: 2. Of those that a mesh axis runs over, the one named last changes fastest.
Arguments:
- activations: bfloat16 [4096, 8192], P('expert'), may hold values from -6 to 6
- out_grad: bfloat16 [4096, 8192], P('expert'), may hold values from -1.5 to 1.5
- expert_ids: int32 [4096, 2], P('expert'), may hold values from 0 to 31, all different within a row; in each aligned block of 128 rows (0 to 127, 128 to 255, ...) at most 16 rows name the same one
- gate_probs: float32 [4096, 2], P('expert'), may hold values from 0.1 to 1
- keep_mask: int32 [4096, 2], P('expert'), may hold values 0 or 1
- w_input: bfloat16 [32, 8192, 1024], P('expert', None, 'mp'), may hold values from -0.1875 to 0.1875
- w_output: bfloat16 [32, 1024, 8192], P('expert', 'mp'), may hold values from -0.0625 to 0.0625
Outputs:
- grad_tokens: bfloat16 [4096, 8192], P('expert', 'mp')
- grad_win: bfloat16 [32, 8192, 1024], P('expert', None, 'mp')
- grad_wout: bfloat16 [32, 1024, 8192], P('expert', 'mp')
Inputs may be any that keep to these rules, and one draw needn't show every extreme that they name: `expert_ids`: each token names two different experts. Within each aligned block of 128 tokens no expert is named by more than 16 tokens, a bound that some block reaches.
All inputs are finite; a program needn't handle non-finite values. No bound on the sum of `keep_mask` on one device may be relied on, other than what follows from the above.
Results may differ from a plain program's by a relative error of at most 0.019.
Values may be sent and summed in bfloat16 or wider, within the bound.
A program may use at most 128 MiB of HBM per device.

v0:
```python
import jax
import jax.numpy as jnp
from jax import lax
from jax.sharding import PartitionSpec as P


def contract_rows(left, right, precision=None):
    return lax.dot_general(
        left,
        right,
        (((0,), (0,)), ((), ())),
        precision=precision,
        preferred_element_type=jnp.float32,
    )


def contract_cols(left, right):
    return lax.dot_general(
        left, right, (((1,), (1,)), ((), ())), preferred_element_type=jnp.float32
    )


def slot_rows(expert_ids, experts, capacity):
    flat = expert_ids.reshape(-1)
    chosen = (flat[:, None] == jnp.arange(experts, dtype=jnp.int32)[None, :]).astype(jnp.int32)
    earlier = jnp.cumsum(chosen, axis=0) - 1
    slots = jnp.sum(chosen * earlier, axis=1).reshape(expert_ids.shape)
    return expert_ids * capacity + slots


def selectors(places, rows_total):
    lanes = jnp.arange(rows_total, dtype=jnp.int32)[:, None]
    return [(places[:, member][None, :] == lanes).astype(jnp.bfloat16) for member in range(2)]


def build_rows(selects, weights_k, source_x, source_g, experts, capacity):
    buffer_x = jnp.zeros((selects[0].shape[0], source_x.shape[1]), jnp.float32)
    buffer_g = jnp.zeros_like(buffer_x)
    grad_wide = source_g.astype(jnp.float32)
    for member in range(2):
        scaled = (weights_k[:, member : member + 1] * grad_wide).astype(jnp.bfloat16)
        buffer_x = buffer_x + jnp.dot(selects[member], source_x, preferred_element_type=jnp.float32)
        buffer_g = buffer_g + jnp.dot(selects[member], scaled, preferred_element_type=jnp.float32)
    shape_out = (experts, capacity, source_x.shape[1])
    return (
        buffer_x.astype(jnp.bfloat16).reshape(shape_out),
        buffer_g.astype(jnp.bfloat16).reshape(shape_out),
    )


def local(activations, out_grad, expert_ids, gate_probs, keep_mask, w_input, w_output):
    experts = lax.axis_size("expert") * w_input.shape[0]
    tok_rows = activations.shape[0]
    model_dim = activations.shape[1]
    capacity = 4 * tok_rows // experts
    places = slot_rows(expert_ids, experts, capacity)
    selects = selectors(places, experts * capacity)
    weights_k = gate_probs * keep_mask.astype(jnp.float32)
    sent_x, sent_g = build_rows(selects, weights_k, activations, out_grad, experts, capacity)
    recv_x, recv_g = (
        lax.all_to_all(sent_x, "expert", split_axis=0, concat_axis=0, tiled=True),
        lax.all_to_all(sent_g, "expert", split_axis=0, concat_axis=0, tiled=True),
    )
    rows_x = recv_x.reshape(-1, model_dim)
    rows_g = recv_g.reshape(-1, model_dim)
    weight_in = w_input[0]
    weight_out = w_output[0]
    hidden = jnp.dot(rows_x, weight_in, preferred_element_type=jnp.float32)
    active, pullback = jax.vjp(jax.nn.gelu, hidden)
    active = active.astype(jnp.bfloat16)
    grad_wout = contract_rows(active, rows_g).astype(jnp.bfloat16)
    grad_act = contract_cols(rows_g, weight_out)
    grad_hidden = pullback(grad_act)[0].astype(jnp.bfloat16)
    grad_win = contract_rows(rows_x, grad_hidden).astype(jnp.bfloat16)
    grad_rows = contract_cols(grad_hidden, weight_in).astype(jnp.bfloat16)
    returned = lax.all_to_all(
        grad_rows.reshape(experts, capacity, model_dim),
        "expert",
        split_axis=0,
        concat_axis=0,
        tiled=True,
    )
    returned = returned.reshape(experts * capacity, model_dim)
    total = jnp.zeros((tok_rows, model_dim), jnp.float32)
    for member in range(2):
        total = total + contract_rows(selects[member], returned)
    grad_tokens = lax.psum_scatter(
        total.astype(jnp.bfloat16), "mp", scatter_dimension=1, tiled=True
    )
    return (grad_tokens, grad_win[None], grad_wout[None])


def solution(mesh):
    return jax.shard_map(
        local,
        mesh=mesh,
        in_specs=(
            P("expert", None),
            P("expert", None),
            P("expert", None),
            P("expert", None),
            P("expert", None),
            P("expert", None, "mp"),
            P("expert", "mp", None),
        ),
        out_specs=(P("expert", "mp"), P("expert", None, "mp"), P("expert", "mp", None)),
        check_vma=False,
    )
```

profile of v0, /device:TPU:1, one launch (start us, length us, event | category | flops | bytes accessed | tf_op | source)
XLA Modules:
  0.0 676.5 jit_solution(6389460994641484444)
XLA Ops:
  7.2 0.0 copy-start
  7.2 0.9 copy.20
  8.1 0.1 eq.59
  8.3 0.1 eq.55
  8.4 0.6 reduce-window.6
  9.0 0.2 slice_reduce_fusion
  9.2 0.1 fusion.37
  9.3 0.1 reshape.49
  9.5 0.1 copy.23
  9.5 0.7 multiply_add_fusion
  10.3 0.0 copy-done
  10.3 8.0 %fusion.25 = f32[512,8192]{1,0:T(8,128)} fusion(bf16[128,8192]{1,0:T(8,128)(2,1)S(1)} %copy-done, s32[128]{0:T(128)S(1)} %get-tuple-element.6), kind=kOutput, calls=%fused_computation.34 | convolution fusion | flops 1073807360 | bytes 18874880 | tf_op jit(solution)/shard_map/dot_general | solution.py:42
  18.3 11.3 %add_convert_fusion = bf16[512,8192]{1,0:T(8,128)(2,1)} fusion(f32[512,8192]{1,0:T(8,128)} %fusion.25, bf16[128,8192]{1,0:T(8,128)(2,1)S(1)} %copy-done, s32[128]{0:T(128)S(1)} %get-tuple-element.5), kind=kOutput, calls=%fused_computation | convolution fusion | flops 1082195968 | bytes 27263488 | tf_op jit(solution)/shard_map/dot_general | solution.py:42
  29.6 12.1 %all-to-all-start.1 = ((bf16[32,16,8192]{2,1,0:T(8,128)(2,1)}), bf16[32,16,8192]{2,1,0:T(8,128)(2,1)}, u32[]{:S(2)}, u32[]{:S(2)}) async-start(bf16[32,16,8192]{2,1,0:T(8,128)(2,1)} %bitcast.56), calls=%async_computation.1 | async-start | bytes 16777216 | tf_op jit(solution)/shard_map/all_to_all | solution.py:61
  41.8 0.0 copy-done.4
  41.8 2.4 fusion.6
  44.2 4.9 add_convert_fusion.1
  49.2 180.9 %all-to-all-done.1 = bf16[32,16,8192]{2,1,0:T(8,128)(2,1)} async-done(((bf16[32,16,8192]{2,1,0:T(8,128)(2,1)}), bf16[32,16,8192]{2,1,0:T(8,128)(2,1)}, u32[]{:S(2)}, u32[]{:S(2)}) %all-to-all-start.1) | async-done | bytes 8388640 | tf_op jit(solution)/shard_map/all_to_all | solution.py:61
  230.1 14.0 %all-to-all-start = ((bf16[32,16,8192]{2,1,0:T(8,128)(2,1)}), bf16[32,16,8192]{2,1,0:T(8,128)(2,1)}, u32[]{:S(2)}, u32[]{:S(2)}) async-start(bf16[32,16,8192]{2,1,0:T(8,128)(2,1)} %bitcast.55), calls=%async_computation | async-start | bytes 16777216 | tf_op jit(solution)/shard_map/all_to_all | solution.py:62
  244.0 0.2 reduce-scatter.2.cloned.1.call-start
  244.3 5.7 fusion.9
  250.0 178.2 %all-to-all-done = bf16[32,16,8192]{2,1,0:T(8,128)(2,1)} async-done(((bf16[32,16,8192]{2,1,0:T(8,128)(2,1)}), bf16[32,16,8192]{2,1,0:T(8,128)(2,1)}, u32[]{:S(2)}, u32[]{:S(2)}) %all-to-all-start) | async-done | bytes 8388640 | tf_op jit(solution)/shard_map/all_to_all | solution.py:62
  428.1 6.3 fusion.21
  434.5 2.3 convolution_convert_fusion
  436.8 194.6 %all_to_all.15 = bf16[32,16,8192]{2,1,0:T(8,128)(2,1)S(1)} all-to-all(bf16[32,16,8192]{2,1,0:T(8,128)(2,1)S(1)} %bitcast.57), channel_id=1, replica_groups=mesh['expert'=32,'mp'=8] {'expert'}, dimensions={0} | all-to-all | bytes 16777216 | tf_op jit(solution)/shard_map/all_to_all | solution.py:76
  631.4 1.3 fusion.24
  632.7 3.2 fusion
  635.9 0.0 reduce-scatter.2.cloned.1.call-update
  635.9 0.0 copy-start.1
  635.9 6.2 fusion.2
  642.2 7.1 %fusion.1 = bf16[1,8192,128]{2,1,0:T(8,128)(2,1)} fusion(bf16[512,8192]{1,0:T(8,128)(2,1)} %bitcast.9, bf16[512,128]{1,0:T(8,128)(2,1)S(1)} %fusion.21), kind=kOutput, calls=%fused_computation.7 | convolution fusion | flops 1074790400 | bytes 10616832 | tf_op jit(solution)/shard_map/dot_general | solution.py:8
  649.3 20.4 %reduce-scatter.2.cloned.1.call-done = bf16[128,1024]{1,0:T(8,128)(2,1)} async-done(((bf16[128,8192]{1,0:T(8,128)(2,1)}), bf16[128,1024]{1,0:T(8,128)(2,1)}) %reduce-scatter.2.cloned.1.call-update) | async-done | bytes 262160 | tf_op jit(solution)/shard_map/reduce_scatter | solution.py:87
  (14 shorter events, 0.1 us)
Async XLA Ops:
  7.2 3.1 copy-start
  29.6 12.2 %copy-start.4 = (f32[128,2]{0,1:T(2,128)S(1)}, f32[128,2]{0,1:T(2,128)}, u32[]{:S(2)}) copy-start(f32[128,2]{0,1:T(2,128)} %param.10) | copy-start | bytes 3076
  29.6 12.2 %copy-start.5 = (s32[128,2]{0,1:T(2,128)S(1)}, s32[128,2]{0,1:T(2,128)}, u32[]{:S(2)}) copy-start(s32[128,2]{0,1:T(2,128)} %param.11) | copy-start | bytes 3076
  29.6 12.2 %copy-start.2 = (bf16[128,8192]{1,0:T(8,128)(2,1)S(1)}, bf16[128,8192]{1,0:T(8,128)(2,1)}, u32[]{:S(2)}) copy-start(bf16[128,8192]{1,0:T(8,128)(2,1)} %param.8) | copy-start | bytes 6291460
  29.6 200.4 %all-to-all-start.1 = ((bf16[32,16,8192]{2,1,0:T(8,128)(2,1)}), bf16[32,16,8192]{2,1,0:T(8,128)(2,1)}, u32[]{:S(2)}, u32[]{:S(2)}) async-start(bf16[32,16,8192]{2,1,0:T(8,128)(2,1)} %bitcast.56), calls=%async_computation.1 | async-start | bytes 16777216 | tf_op jit(solution)/shard_map/all_to_all | solution.py:61
  230.1 14.2 %copy-start.3 = (bf16[1,8192,128]{2,1,0:T(8,128)(2,1)S(1)}, bf16[1,8192,128]{2,1,0:T(8,128)(2,1)}, u32[]{:S(2)}) copy-start(bf16[1,8192,128]{2,1,0:T(8,128)(2,1)} %param.12) | copy-start | bytes 6291460
  230.1 198.1 %all-to-all-start = ((bf16[32,16,8192]{2,1,0:T(8,128)(2,1)}), bf16[32,16,8192]{2,1,0:T(8,128)(2,1)}, u32[]{:S(2)}, u32[]{:S(2)}) async-start(bf16[32,16,8192]{2,1,0:T(8,128)(2,1)} %bitcast.55), calls=%async_computation | async-start | bytes 16777216 | tf_op jit(solution)/shard_map/all_to_all | solution.py:62
  244.0 425.6 %reduce-scatter.2.cloned.1.call-start = ((), (), s32[]{:S(2)}) async-start(), calls=%async_computation.4 | async-start | bytes 2359296 | tf_op jit(solution)/shard_map/reduce_scatter | solution.py:87
  635.9 33.7 %copy-start.1 = (bf16[128,8192]{1,0:T(8,128)(2,1)S(1)}, bf16[128,8192]{1,0:T(8,128)(2,1)}, u32[]{:S(2)}) copy-start(bf16[128,8192]{1,0:T(8,128)(2,1)} %param.7) | copy-start | bytes 6291460
Sparse Core Ops, SparseCore 0:
  636.1 33.5 reduce-scatter.1
where the time goes:
time: 679 us; the launch traced here: 676 us
  waiting for transfers between devices  379 us (56%)
  blocking collectives  195 us (29%)
  matrix products  58.9 us (9%)
  starting transfers between devices  26.3 us (4%)
  between operations  14.2 us (2%)
    all_to_all x1, blocking collectives, local(): lax.all_to_all(grad_rows.reshape(experts, capacity, model_dim), 'expert',...  195 us
    all_to_all x1, waiting for transfers between devices, local(): lax.all_to_all(sent_x, 'expert', split_axis=0, concat_axis=0, tiled=True)  181 us
    all_to_all x1, waiting for transfers between devices, local(): lax.all_to_all(sent_g, 'expert', split_axis=0, concat_axis=0, tiled=True)  178 us
    reduce_scatter x1, waiting for transfers between devices, local(): lax.psum_scatter(total.astype(jnp.bfloat16), 'mp', scatter_dimension=1, t...  20.4 us
    dot_general x2, matrix products, build_rows(): jnp.dot(selects[member], source_x, preferred_element_type=jnp.float32)  19.3 us
    dot_general x4, matrix products, contract_rows(): lax.dot_general(left, right, (((0,), (0,)), ((), ())), precision=precisio...  17.8 us
    all_to_all x1, starting transfers between devices, local(): lax.all_to_all(sent_g, 'expert', split_axis=0, concat_axis=0, tiled=True)  14 us
  transfers between devices with their start and end apart: 3, of which 3 were waited for; matrix products, arithmetic and copies ran while one was open for 4% of the time, Pallas kernels for 0%

commit v1 on v0

v1 whole, which is shorter than its diff:
```python
import jax
import jax.numpy as jnp
from jax import lax
from jax.sharding import PartitionSpec as P


def contract_rows(left, right):
    return lax.dot_general(
        left, right, (((0,), (0,)), ((), ())), preferred_element_type=jnp.float32
    )


def contract_cols(left, right):
    return lax.dot_general(
        left, right, (((1,), (1,)), ((), ())), preferred_element_type=jnp.float32
    )


def slot_rows(expert_ids, experts, capacity):
    flat = expert_ids.reshape(-1)
    chosen = (flat[:, None] == jnp.arange(experts, dtype=jnp.int32)[None, :]).astype(jnp.int32)
    earlier = jnp.cumsum(chosen, axis=0) - 1
    slots = jnp.sum(chosen * earlier, axis=1).reshape(expert_ids.shape)
    return expert_ids * capacity + slots


def local(activations, out_grad, expert_ids, gate_probs, keep_mask, w_input, w_output):
    experts = lax.axis_size("expert")
    parts = lax.axis_size("mp")
    me = lax.axis_index("mp")
    tok_rows, model_dim = activations.shape
    width = model_dim // parts
    capacity = 4 * tok_rows // experts
    rows_total = experts * capacity
    places = slot_rows(expert_ids, experts, capacity)
    lanes = jnp.arange(rows_total, dtype=jnp.int32)[:, None]
    hit = [places[:, k][None, :] == lanes for k in range(2)]
    select = (hit[0] | hit[1]).astype(jnp.bfloat16)
    weights_k = gate_probs * keep_mask.astype(jnp.float32)
    factor = sum(
        jnp.sum(jnp.where(hit[k], weights_k[:, k][None, :], 0.0), axis=1, keepdims=True)
        for k in range(2)
    )
    mine_x = lax.dynamic_slice(activations, (0, me * width), (tok_rows, width))
    mine_g = lax.dynamic_slice(out_grad, (0, me * width), (tok_rows, width))
    sent_x = jnp.dot(select, mine_x, preferred_element_type=jnp.float32).astype(jnp.bfloat16)
    sent_g = (factor * jnp.dot(select, mine_g, preferred_element_type=jnp.float32)).astype(jnp.bfloat16)
    sent = jnp.stack([sent_x, sent_g], axis=1).reshape(experts, capacity * 2 * width // 128, 128)
    recv = lax.all_to_all(sent, "expert", split_axis=0, concat_axis=0, tiled=True)
    recv = recv.reshape(rows_total, 2, width)
    rows_x = lax.all_gather(recv[:, 0], "mp", axis=1, tiled=True)
    rows_g = lax.all_gather(recv[:, 1], "mp", axis=1, tiled=True)
    weight_in = w_input[0]
    weight_out = w_output[0]
    hidden = jnp.dot(rows_x, weight_in, preferred_element_type=jnp.float32)
    active, pullback = jax.vjp(jax.nn.gelu, hidden)
    active = active.astype(jnp.bfloat16)
    grad_wout = contract_rows(active, rows_g).astype(jnp.bfloat16)
    grad_act = contract_cols(rows_g, weight_out)
    grad_hidden = pullback(grad_act)[0].astype(jnp.bfloat16)
    grad_win = contract_rows(rows_x, grad_hidden).astype(jnp.bfloat16)
    grad_rows = contract_cols(grad_hidden, weight_in).astype(jnp.bfloat16)
    summed = lax.psum_scatter(grad_rows, "mp", scatter_dimension=1, tiled=True)
    returned = lax.all_to_all(
        summed.reshape(experts, capacity, width), "expert", split_axis=0, concat_axis=0, tiled=True
    ).reshape(rows_total, width)
    grad_tokens = contract_rows(select, returned).astype(jnp.bfloat16)
    return (grad_tokens, grad_win[None], grad_wout[None])


def solution(mesh):
    return jax.shard_map(
        local,
        mesh=mesh,
        in_specs=(
            P("expert", None),
            P("expert", None),
            P("expert", None),
            P("expert", None),
            P("expert", None),
            P("expert", None, "mp"),
            P("expert", "mp", None),
        ),
        out_specs=(P("expert", "mp"), P("expert", None, "mp"), P("expert", "mp", None)),
        check_vma=False,
    )
```

time: 679 us -> 313 us (0.46)
  waiting for transfers between devices: 379 us -> 165 us
  blocking collectives: 195 us -> 59.1 us
  matrix products: 58.9 us -> 34.6 us
  local copies, waits for them, and re-layouts: 1.65 us -> 24.4 us
  starting transfers between devices: 26.3 us -> 9.84 us
    all_to_all x2 -> x1, waiting for transfers between devices: 359 us -> 11.5 us  [local(): lax.all_to_all(summed.reshape(experts, capacity, width), 'expert', split_...]
    all_to_all x1, blocking collectives: 195 us -> 59.1 us  [local(): lax.all_to_all(sent, 'expert', split_axis=0, concat_axis=0, tiled=True)]
    all_gather x0 -> x2, waiting for transfers between devices: none -> 99.3 us  [the longest x1 50.6 us: local(): rows_x = lax.all_gather(recv[:, 0], 'mp', axis=1, tiled=True)]
    reduce_scatter x1, waiting for transfers between devices: 20.4 us -> 54.3 us  [local(): summed = lax.psum_scatter(grad_rows, 'mp', scatter_dimension=1, tiled=True)]
    dot_general x8 -> x5, matrix products: 44.5 us -> 17 us  [the longest x3 14.3 us: contract_rows(): lax.dot_general(left, right, (((0,), (0,)), ((), ())), preferred_element_...]
    all_to_all x2 -> x1, starting transfers between devices: 26.1 us -> 9.54 us  [local(): lax.all_to_all(summed.reshape(experts, capacity, width), 'expert', split_...]
    reshape x0 -> x2, local copies, waits for them, and re-layouts: none -> 8.32 us  [the longest x1 4.37 us: local(): jnp.stack([sent_x, sent_g], axis=1)]
  transfers between devices with their start and end apart: 3 -> 4, of which waited for: 3 -> 4; matrix products, arithmetic and copies ran while one was open for 4% -> 7% of each run, Pallas kernels for 0% -> 0%
where the time goes in v1:
time: 313 us; the launch traced here: 309 us
  waiting for transfers between devices  165 us (53%)
  blocking collectives  59.1 us (19%)
  matrix products  34.6 us (11%)
  local copies, waits for them, and re-layouts  24.4 us (8%)
  between operations  13.8 us (4%)
  starting transfers between devices  9.84 us (3%)
    all_to_all x1, blocking collectives, local(): lax.all_to_all(sent, 'expert', split_axis=0, concat_axis=0, tiled=True)  59.1 us
    reduce_scatter x1, waiting for transfers between devices, local(): summed = lax.psum_scatter(grad_rows, 'mp', scatter_dimension=1, tiled=True)  54.3 us
    all_gather x1, waiting for transfers between devices, local(): rows_x = lax.all_gather(recv[:, 0], 'mp', axis=1, tiled=True)  50.6 us
    all_gather x1, waiting for transfers between devices, local(): rows_g = lax.all_gather(recv[:, 1], 'mp', axis=1, tiled=True)  48.6 us
    dot_general x3, matrix products, contract_rows(): lax.dot_general(left, right, (((0,), (0,)), ((), ())), preferred_element_...  14.3 us
    dot_general x2, matrix products, contract_cols(): lax.dot_general(left, right, (((1,), (1,)), ((), ())), preferred_element_...  11.9 us
    all_to_all x1, waiting for transfers between devices, local(): lax.all_to_all(summed.reshape(experts, capacity, width), 'expert', split_...  11.5 us
    all_to_all x1, starting transfers between devices, local(): lax.all_to_all(summed.reshape(experts, capacity, width), 'expert', split_...  9.54 us
  transfers between devices with their start and end apart: 4, of which 4 were waited for; matrix products, arithmetic and copies ran while one was open for 7% of the time, Pallas kernels for 0%

profile of v1, /device:TPU:1, one launch (start us, length us, event | category | flops | bytes accessed | tf_op | source)
XLA Modules:
  0.0 309.4 jit_solution(2373680340636574936)
XLA Ops:
  7.2 0.9 copy.34
  8.2 0.1 eq.59
  8.3 0.1 eq.55
  8.4 0.7 convert_multiply_fusion
  9.2 0.6 reduce-window.6
  9.7 0.2 slice_reduce_fusion
  10.0 0.1 fusion.41
  10.1 0.1 reshape.51
  10.3 0.7 multiply_add_fusion
  11.0 0.2 select_reduce_fusion
  11.2 1.4 fusion.12
  12.6 1.4 fusion.11
  14.0 0.2 pad_maximum_fusion
  14.2 3.5 %copy.38 = bf16[512,2,1024]{2,1,0:T(2,128)(2,1)} copy(bf16[512,2,1024]{2,0,1:T(8,128)(2,1)S(1)} %pad_maximum_fusion) | data formatting | bytes 4194304 | tf_op jit(solution)/shard_map/stack | solution.py:48
  17.7 4.4 %reshape.52 = bf16[32,256,128]{2,1,0:T(8,128)(2,1)} reshape(bf16[512,2,1024]{2,1,0:T(2,128)(2,1)} %copy.38) | data formatting | bytes 4194304 | tf_op jit(solution)/shard_map/reshape | solution.py:48
  22.1 59.1 %all_to_all.10 = bf16[32,256,128]{2,1,0:T(8,128)(2,1)} all-to-all(bf16[32,256,128]{2,1,0:T(8,128)(2,1)} %reshape.52), channel_id=1, replica_groups=mesh['expert'=32,'mp'=8] {'expert'}, dimensions={0} | all-to-all | bytes 4194304 | tf_op jit(solution)/shard_map/all_to_all | solution.py:49
  81.1 4.0 %reshape.53 = bf16[512,2,1024]{2,1,0:T(2,128)(2,1)} reshape(bf16[32,256,128]{2,1,0:T(8,128)(2,1)} %all_to_all.10) | data formatting | bytes 4194304 | tf_op jit(solution)/shard_map/reshape | solution.py:50
  85.1 6.7 %fusion.49 = (bf16[512,1,1024]{2,1,0:T(2,128)(2,1)}, bf16[512,1,1024]{2,1,0:T(2,128)(2,1)S(1)}) fusion(bf16[512,2,1024]{2,1,0:T(2,128)(2,1)} %reshape.53), kind=kLoop, calls=%fused_computation.67 | loop fusion | bytes 4194304 | tf_op jit(solution)/shard_map/slice | solution.py:52
  91.7 1.3 copy.42
  93.2 3.0 copy.41
  96.1 0.2 reduce-scatter.2.cloned.1.call-start
  96.4 50.6 %all-gather.7.cloned.1.call-done = bf16[512,1,8192]{2,0,1:T(8,128)(2,1)} async-done(((bf16[512,1,1024]{2,0,1:T(8,128)(2,1)}), bf16[512,1,8192]{2,0,1:T(8,128)(2,1)}) %all-gather.7.cloned.1.call-update) | async-done | bytes 8388624 | tf_op jit(solution)/shard_map/all_gather | solution.py:51
  147.0 5.7 %fusion.3 = f32[512,128]{1,0:T(8,128)S(1)} fusion(bf16[512,1,8192]{2,0,1:T(8,128)(2,1)} %all-gather.7.cloned.1.call-done, bf16[1,8192,128]{2,1,0:T(8,128)(2,1)S(1)} %copy-done), kind=kOutput, calls=%fused_computation.6 | convolution fusion | flops 1073741824 | bytes 10747904 | tf_op jit(solution)/shard_map/dot_general | solution.py:55
  152.7 48.6 %all-gather.5.cloned.1.call-done = bf16[512,1,8192]{2,0,1:T(8,128)(2,1)} async-done(((bf16[512,1,1024]{2,0,1:T(8,128)(2,1)}), bf16[512,1,8192]{2,0,1:T(8,128)(2,1)}) %all-gather.5.cloned.1.call-update) | async-done | bytes 8388624 | tf_op jit(solution)/shard_map/all_gather | solution.py:52
  201.4 6.3 %fusion.19 = bf16[512,128]{1,0:T(8,128)(2,1)S(1)} fusion(f32[512,128]{1,0:T(8,128)S(1)} %fusion.3, bf16[1,128,8192]{2,1,0:T(8,128)(2,1)} %param.13, bf16[512,1,8192]{2,0,1:T(8,128)(2,1)} %all-gather.5.cloned.1.call-done), kind=kOutput, calls=%fused_computation.28 | convolution fusion | flops 1075052544 | bytes 10878976 | tf_op jit(solution)/shard_map/dot_general | solution.py:14
  207.7 5.6 %convolution_convert_fusion = bf16[512,8192]{1,0:T(8,128)(2,1)} fusion(bf16[512,128]{1,0:T(8,128)(2,1)S(1)} %fusion.19, bf16[1,8192,128]{2,1,0:T(8,128)(2,1)S(1)} %copy-done), kind=kOutput, calls=%fused_computation | convolution fusion | flops 1077936128 | bytes 10616832 | tf_op jit(solution)/shard_map/dot_general | solution.py:14
  213.3 54.3 %reduce-scatter.2.cloned.1.call-done = bf16[512,1024]{1,0:T(8,128)(2,1)} async-done(((bf16[512,8192]{1,0:T(8,128)(2,1)}), bf16[512,1024]{1,0:T(8,128)(2,1)}) %reduce-scatter.2.cloned.1.call-update) | async-done | bytes 1048592 | tf_op jit(solution)/shard_map/reduce_scatter | solution.py:63
  267.6 9.5 %all-to-all-start.1 = ((bf16[32,16,1024]{2,1,0:T(8,128)(2,1)}), bf16[32,16,1024]{2,1,0:T(8,128)(2,1)S(1)}, u32[]{:S(2)}, u32[]{:S(2)}) async-start(bf16[32,16,1024]{2,1,0:T(8,128)(2,1)} %bitcast.59), calls=%async_computation.2 | async-start | bytes 2097152 | tf_op jit(solution)/shard_map/all_to_all | solution.py:64
  277.2 6.1 %fusion.1 = bf16[1,128,8192]{2,1,0:T(8,128)(2,1)} fusion(bf16[512,1,8192]{2,0,1:T(8,128)(2,1)} %all-gather.5.cloned.1.call-done, f32[512,128]{1,0:T(8,128)S(1)} %fusion.3), kind=kOutput, calls=%fused_computation.4 | convolution fusion | flops 1075380224 | bytes 10747904 | tf_op jit(solution)/shard_map/dot_general | solution.py:8
  283.3 7.1 %fusion = bf16[1,8192,128]{2,1,0:T(8,128)(2,1)} fusion(bf16[512,128]{1,0:T(8,128)(2,1)S(1)} %fusion.19, bf16[512,1,8192]{2,0,1:T(8,128)(2,1)} %all-gather.7.cloned.1.call-done), kind=kOutput, calls=%fused_computation.3 | convolution fusion | flops 1074790400 | bytes 10616832 | tf_op jit(solution)/shard_map/dot_general | solution.py:8
  290.4 11.5 %all-to-all-done.1 = bf16[32,16,1024]{2,1,0:T(8,128)(2,1)S(1)} async-done(((bf16[32,16,1024]{2,1,0:T(8,128)(2,1)}), bf16[32,16,1024]{2,1,0:T(8,128)(2,1)S(1)}, u32[]{:S(2)}, u32[]{:S(2)}) %all-to-all-start.1) | async-done | bytes 1048608 | tf_op jit(solution)/shard_map/all_to_all | solution.py:64
  301.9 1.1 convolution_convert_fusion.4
  (14 shorter events, 0.3 us)
Async XLA Ops:
  7.2 139.8 %copy-start = (bf16[1,8192,128]{2,1,0:T(8,128)(2,1)S(1)}, bf16[1,8192,128]{2,1,0:T(8,128)(2,1)}, u32[]{:S(2)}) copy-start(bf16[1,8192,128]{2,1,0:T(8,128)(2,1)} %param.12) | copy-start | bytes 6291460
  7.2 139.8 %all-gather.7.cloned.1.call-start = ((), (), s32[]{:S(2)}) async-start(), calls=%async_computation.5 | async-start | bytes 9437184 | tf_op jit(solution)/shard_map/all_gather | solution.py:51
  93.1 108.3 %all-gather.5.cloned.1.call-start = ((), (), s32[]{:S(2)}) async-start(), calls=%async_computation.4 | async-start | bytes 9437184 | tf_op jit(solution)/shard_map/all_gather | solution.py:52
  96.1 171.5 %reduce-scatter.2.cloned.1.call-start = ((), (), s32[]{:S(2)}) async-start(), calls=%async_computation.3 | async-start | bytes 9437184 | tf_op jit(solution)/shard_map/reduce_scatter | solution.py:63
  267.6 34.2 %all-to-all-start.1 = ((bf16[32,16,1024]{2,1,0:T(8,128)(2,1)}), bf16[32,16,1024]{2,1,0:T(8,128)(2,1)S(1)}, u32[]{:S(2)}, u32[]{:S(2)}) async-start(bf16[32,16,1024]{2,1,0:T(8,128)(2,1)} %bitcast.59), calls=%async_computation.2 | async-start | bytes 2097152 | tf_op jit(solution)/shard_map/all_to_all | solution.py:64
Sparse Core Ops, SparseCore 0:
  93.2 53.7 all-gather.6
  148.8 52.4 all-gather.4
  213.4 54.1 reduce-scatter.1

commit v2 on v1

v2 whole, which is shorter than its diff:
```python
import functools
import math
import jax
import jax.numpy as jnp
from jax import lax
from jax.sharding import PartitionSpec as P
import jax.experimental.pallas as pl
import jax.experimental.pallas.tpu as pltpu

CAP = 16
NY = 4
GRID = {32: (4, 8)}
MESH = pl.DeviceIdType.MESH
SCALE = math.sqrt(2.0 / math.pi)
CUBE = 0.044715


def contract_cols(left, right):
    return lax.dot_general(
        left, right, (((1,), (1,)), ((), ())), preferred_element_type=jnp.float32
    )


def product(left, right):
    return jnp.dot(left, right, preferred_element_type=jnp.float32)


def wrap(value, size):
    return lax.rem(value + size, size)


def kernel(
    nx, nz,
    ids_ref, weight_ref, act_hbm, grad_hbm, win_hbm, wout_hbm,
    tokens_out, gwin_hbm, gwout_hbm,
    act_v, grad_v, sent, rows, win_v, wout_v, win_all, hid_grad, active_v,
    back_sent, back, gwin_v, gwout_v,
    load_sem, win_send, win_recv, out_send, out_recv, ring_send, left_recv, right_recv,
    far_recv, core_recv, hid_send, hid_recv, back_send, back_recv, store_sem,
):
    experts = nx * nz
    toks, width = act_v.shape
    parts = rows.shape[0]
    total = sent.shape[0]
    span = nz * CAP
    half = span // 2
    ff = win_v.shape[1]
    me_e = lax.axis_index("expert")
    me_m = lax.axis_index("mp")
    mx, mz = me_e // nz, lax.rem(me_e, nz)
    my, mc = me_m // 2, lax.rem(me_m, 2)

    def expert_at(dx, dz):
        return {"expert": lax.rem(mx + dx, nx) * nz + lax.rem(mz + dz, nz)}

    def mate_at(dy, dc):
        return lax.rem(my + dy, NY) * 2 + lax.rem(mc + dc, 2)

    right, left, far = mate_at(1, 0), mate_at(NY - 1, 0), mate_at(2, 0)
    other = mate_at(0, 1)

    col = pl.multiple_of(me_m * width, width)
    loads = [
        pltpu.make_async_copy(act_hbm.at[:, pl.ds(col, width)], act_v, load_sem.at[0]),
        pltpu.make_async_copy(grad_hbm.at[:, pl.ds(col, width)], grad_v, load_sem.at[1]),
        pltpu.make_async_copy(win_hbm, win_v, load_sem.at[2]),
        pltpu.make_async_copy(wout_hbm, wout_v, load_sem.at[3]),
    ]
    for load in loads:
        load.start()

    barrier = pltpu.get_barrier_semaphore()

    @pl.loop(1, experts)
    def _(step):
        pl.semaphore_signal(
            barrier, inc=1, device_id=expert_at(step // nz, lax.rem(step, nz)), device_id_type=MESH
        )

    @pl.loop(1, parts)
    def _(step):
        pl.semaphore_signal(
            barrier, inc=1, device_id={"mp": lax.rem(me_m + step, parts)}, device_id_type=MESH
        )

    ids = ids_ref[...]
    weights = weight_ref[...]
    lane_e = lax.broadcasted_iota(jnp.int32, (experts, toks), 0)
    chosen = [(lane_e == ids[k : k + 1, :]).astype(jnp.float32) for k in range(2)]
    before = lax.broadcasted_iota(jnp.int32, (toks, toks), 0)
    after = lax.broadcasted_iota(jnp.int32, (toks, toks), 1)
    upper = (before < after).astype(jnp.bfloat16)
    earlier = product((chosen[0] + chosen[1]).astype(jnp.bfloat16), upper)
    dx = (ids >> int(math.log2(nz))) - mx
    dx = jnp.where(dx < 0, dx + nx, dx)
    dz = (ids & (nz - 1)) - mz
    dz = jnp.where(dz < 0, dz + nz, dz)
    base = (dx * nz + dz) * CAP
    places = [
        base[k : k + 1, :]
        + jnp.sum(chosen[k] * earlier, axis=0, keepdims=True).astype(jnp.int32)
        for k in range(2)
    ]

    def select(start, count):
        lanes = lax.broadcasted_iota(jnp.int32, (count, toks), 0) + start
        hit = [lanes == places[k] for k in range(2)]
        picked = jnp.logical_or(hit[0], hit[1])
        factor = jnp.where(hit[0], weights[0:1, :], 0.0) + jnp.where(hit[1], weights[1:2, :], 0.0)
        return picked, jnp.sum(factor, axis=1, keepdims=True)

    pl.semaphore_wait(barrier, experts - 1 + parts - 1)

    keep_win = pltpu.make_async_copy(
        win_hbm.at[pl.ds(col, width)], win_all.at[me_m], win_recv
    )
    keep_win.start()

    @pl.loop(1, parts)
    def _(step):
        mate = lax.rem(me_m + step, parts)
        start = pl.multiple_of(mate * width, width)
        pltpu.make_async_remote_copy(
            win_hbm.at[pl.ds(start, width)], win_all.at[me_m], win_send, win_recv,
            device_id={"mp": mate}, device_id_type=MESH,
        ).start()

    loads[0].wait()
    loads[1].wait()
    for k in range(nx):
        first = k * span
        picked, factor = select(first, span)
        picked = picked.astype(jnp.float32).astype(jnp.bfloat16)
        sent[pl.ds(first, span), pl.ds(0, width)] = product(picked, act_v[...]).astype(jnp.bfloat16)
        sent[pl.ds(first, span), pl.ds(width, width)] = (
            factor * product(picked, grad_v[...])
        ).astype(jnp.bfloat16)
        if k == 0:
            pltpu.make_async_copy(
                sent.at[pl.ds(0, CAP)], rows.at[me_m, pl.ds(0, CAP)], out_recv.at[0]
            ).start()

        @pl.loop(1 if k == 0 else 0, nz)
        def _(step):
            at = pl.ds(pl.multiple_of(first + step * CAP, CAP), CAP)
            pltpu.make_async_remote_copy(
                sent.at[at], rows.at[me_m, at], out_send.at[k], out_recv.at[k],
                device_id=expert_at(k, step), device_id_type=MESH,
            ).start()

    ring = []

    def pass_on(kind, k, slot, start, count, recv, mate):
        copy = pltpu.make_async_remote_copy(
            rows.at[slot, pl.ds(start, count)], rows.at[slot, pl.ds(start, count)],
            ring_send.at[kind, k], recv, device_id={"mp": mate}, device_id_type=MESH,
        )
        copy.start()
        ring.append(copy)

    def arrived(ref, sem):
        pltpu.make_async_copy(ref, ref, sem).wait()

    def stage_own(k):
        at = k * span
        arrived(rows.at[me_m, pl.ds(at, span)], out_recv.at[k])
        pass_on(0, k, me_m, at, span, left_recv.at[k], right)
        pass_on(1, k, me_m, at, span, right_recv.at[k], left)
        pass_on(2, k, me_m, at, span, core_recv.at[k], other)

    def stage_near(k):
        at = k * span
        arrived(rows.at[left, pl.ds(at, span)], left_recv.at[k])
        pass_on(3, k, left, at, half, far_recv.at[0, k], right)
        pass_on(4, k, left, at, span, core_recv.at[k], other)
        arrived(rows.at[right, pl.ds(at, span)], right_recv.at[k])
        pass_on(5, k, right, at + half, half, far_recv.at[1, k], left)
        pass_on(6, k, right, at, span, core_recv.at[k], other)

    def stage_far(k):
        at = k * span
        arrived(rows.at[far, pl.ds(at, half)], far_recv.at[0, k])
        arrived(rows.at[far, pl.ds(at + half, half)], far_recv.at[1, k])
        pass_on(7, k, far, at, span, core_recv.at[k], other)

    def stage_hidden(k):
        at = k * span
        arrived(rows.at[pl.ds(0, NY), pl.ds(at, span)], core_recv.at[k])
        if k == 0:
            loads[2].wait()
            loads[3].wait()

        def add(part, sums):
            hidden, grad_act = sums
            here = pl.ds(pl.multiple_of(part * width, width), width)
            block = rows[part, pl.ds(at, span), :]
            hidden = hidden + product(block[:, :width], win_v[here, :])
            grad_act = grad_act + contract_cols(block[:, width:], wout_v[:, here])
            return hidden, grad_act

        zero = jnp.zeros((span, ff), jnp.float32)
        hidden, grad_act = lax.fori_loop(0, parts, add, (zero, zero))
        square = hidden * hidden
        tanh = jnp.tanh(SCALE * (hidden + CUBE * (square * hidden)))
        active = 0.5 * hidden * (1.0 + tanh)
        slope = 0.5 * (1.0 + tanh) + 0.5 * hidden * (1.0 - tanh * tanh) * (
            SCALE * (1.0 + 3.0 * CUBE * square)
        )
        active_v[pl.ds(at, span), :] = active.astype(jnp.bfloat16)
        hid_grad[me_m, pl.ds(at, span), :] = (grad_act * slope).astype(jnp.bfloat16)

        @pl.loop(1, parts)
        def _(step):
            pltpu.make_async_remote_copy(
                hid_grad.at[me_m, pl.ds(at, span)], hid_grad.at[me_m, pl.ds(at, span)],
                hid_send.at[k], hid_recv.at[k],
                device_id={"mp": lax.rem(me_m + step, parts)}, device_id_type=MESH,
            ).start()

    def stage_back(k):
        at = k * span
        if k == 0:
            arrived(win_all, win_recv)
        arrived(hid_grad.at[pl.ds(0, parts - 1), pl.ds(at, span)], hid_recv.at[k])
        grads = jnp.concatenate([hid_grad[s, pl.ds(at, span), :] for s in range(parts)], axis=1)
        tile = min(256, width)

        @pl.loop(0, width // tile)
        def _(step):
            here = pl.ds(pl.multiple_of(step * tile, tile), tile)
            block = jnp.concatenate([win_all[s, here, :] for s in range(parts)], axis=1)
            back_sent[pl.ds(at, span), here] = contract_cols(grads, block).astype(jnp.bfloat16)

        if k == 0:
            pltpu.make_async_copy(
                back_sent.at[pl.ds(0, CAP)], back.at[pl.ds(0, CAP)], back_recv
            ).start()

        @pl.loop(1 if k == 0 else 0, nz)
        def _(step):
            here = pl.ds(pl.multiple_of(at + step * CAP, CAP), CAP)
            pltpu.make_async_remote_copy(
                back_sent.at[here], back.at[here], back_send, back_recv,
                device_id=expert_at(nx - k, nz - step), device_id_type=MESH,
            ).start()

    for step in range(nx + 4):
        if step < nx:
            stage_own(step)
        if 0 <= step - 1 < nx:
            stage_near(step - 1)
        if 0 <= step - 2 < nx:
            stage_far(step - 2)
        if 0 <= step - 3 < nx:
            stage_hidden(step - 3)
        if 0 <= step - 4 < nx:
            stage_back(step - 4)

    active_t = active_v[...].astype(jnp.float32).T.astype(jnp.bfloat16)
    hid_t = hid_grad[me_m].astype(jnp.float32).T.astype(jnp.bfloat16)
    tile = min(512, width)

    @pl.loop(0, parts)
    def _(part):
        for piece in range(width // tile):
            here = pl.ds(pl.multiple_of(part * width + piece * tile, tile), tile)
            gwout_v[:, here] = product(
                active_t, rows[part, :, pl.ds(width + piece * tile, tile)]
            ).astype(jnp.bfloat16)
            gwin_v[here, :] = product(
                hid_t, rows[part, :, pl.ds(piece * tile, tile)]
            ).T.astype(jnp.bfloat16)

    stores = [
        pltpu.make_async_copy(gwin_v, gwin_hbm, store_sem.at[0]),
        pltpu.make_async_copy(gwout_v, gwout_hbm, store_sem.at[1]),
    ]
    for store in stores:
        store.start()

    arrived(back, back_recv)
    for k in range(nx):
        picked, _ = select(k * span, span)
        picked_t = picked.astype(jnp.float32).T.astype(jnp.bfloat16)
        term = product(picked_t, back[pl.ds(k * span, span), :])
        sums = term if k == 0 else sums + term
    tokens_out[...] = sums.astype(jnp.bfloat16)

    for k in range(nx):
        lo = CAP if k == 0 else k * span
        gone = sent.at[pl.ds(lo, (k + 1) * span - lo)]
        arrived(gone, out_send.at[k])
        sent_hid = hid_grad.at[pl.ds(0, parts - 1), pl.ds(k * span, span)]
        arrived(sent_hid, hid_send.at[k])
    for copy in ring:
        copy.wait_send()
    arrived(win_all.at[pl.ds(0, parts - 1)], win_send)
    gone = back_sent.at[pl.ds(CAP, total - CAP)]
    arrived(gone, back_send)
    for store in stores:
        store.wait()


def local(grid, activations, out_grad, expert_ids, gate_probs, keep_mask, w_input, w_output):
    nx, nz = grid
    experts = nx * nz
    parts = lax.axis_size("mp")
    toks, model = activations.shape
    width = model // parts
    ff = w_input.shape[2]
    total = experts * CAP
    weights = (gate_probs * keep_mask.astype(jnp.float32)).T
    bf16 = jnp.bfloat16
    vmem = pl.BlockSpec(memory_space=pltpu.VMEM)
    hbm = pl.BlockSpec(memory_space=pl.ANY)
    dma = pltpu.SemaphoreType.DMA
    tokens, gwin, gwout = pl.pallas_call(
        functools.partial(kernel, nx, nz),
        name="moe_backward",
        out_shape=(
            jax.ShapeDtypeStruct((toks, width), bf16),
            jax.ShapeDtypeStruct((model, ff), bf16),
            jax.ShapeDtypeStruct((ff, model), bf16),
        ),
        in_specs=[vmem, vmem, hbm, hbm, hbm, hbm],
        out_specs=(vmem, hbm, hbm),
        scratch_shapes=[
            pltpu.VMEM((toks, width), bf16),
            pltpu.VMEM((toks, width), bf16),
            pltpu.VMEM((total, 2 * width), bf16),
            pltpu.VMEM((parts, total, 2 * width), bf16),
            pltpu.VMEM((model, ff), bf16),
            pltpu.VMEM((ff, model), bf16),
            pltpu.VMEM((parts, width, ff), bf16),
            pltpu.VMEM((parts, total, ff), bf16),
            pltpu.VMEM((total, ff), bf16),
            pltpu.VMEM((total, width), bf16),
            pltpu.VMEM((total, width), bf16),
            pltpu.VMEM((model, ff), bf16),
            pltpu.VMEM((ff, model), bf16),
            dma((4,)),
            dma(()),
            dma(()),
            dma((nx,)),
            dma((nx,)),
            dma((8, nx)),
            dma((nx,)),
            dma((nx,)),
            dma((2, nx)),
            dma((nx,)),
            dma((nx,)),
            dma((nx,)),
            dma(()),
            dma(()),
            dma((2,)),
        ],
        compiler_params=pltpu.CompilerParams(
            collective_id=0, has_side_effects=True, vmem_limit_bytes=48 * 2**20
        ),
        cost_estimate=pl.CostEstimate(
            flops=10 * total * model * ff, bytes_accessed=8 * model * ff * 2, transcendentals=total * ff
        ),
    )(expert_ids.T, weights, activations, out_grad, w_input[0], w_output[0])
    return (tokens, gwin[None], gwout[None])


def solution(mesh):
    grid = GRID[mesh.shape["expert"]]
    return jax.shard_map(
        functools.partial(local, grid),
        mesh=mesh,
        in_specs=(
            P("expert", None),
            P("expert", None),
            P("expert", None),
            P("expert", None),
            P("expert", None),
            P("expert", None, "mp"),
            P("expert", "mp", None),
        ),
        out_specs=(P("expert", "mp"), P("expert", None, "mp"), P("expert", "mp", None)),
        check_vma=False,
    )
```

time: 313 us -> 137 us (0.44); the launches traced: 309 us -> 137 us
  waiting for transfers between devices: 165 us -> 0 us
  Pallas kernels: 0 us -> 132 us
  blocking collectives: 59.1 us -> 0 us
  matrix products: 34.6 us -> 0 us
  local copies, waits for them, and re-layouts: 24.4 us -> 4.02 us
  between operations: 13.8 us -> 0.64 us
  starting transfers between devices: 9.84 us -> 0 us
    pallas_call x0 -> x1, Pallas kernels: none -> 132 us  [local(): pl.pallas_call(functools.partial(kernel, nx, nz), name='moe_backward', ou...]
    all_gather x2 -> x0, waiting for transfers between devices: 99.3 us -> none  [the longest x1 50.6 us: local(): rows_x = lax.all_gather(recv[:, 0], 'mp', axis=1, tiled=True)]
    all_to_all x1 -> x0, blocking collectives: 59.1 us -> none  [local(): lax.all_to_all(sent, 'expert', split_axis=0, concat_axis=0, tiled=True)]
    reduce_scatter x1 -> x0, waiting for transfers between devices: 54.3 us -> none  [local(): summed = lax.psum_scatter(grad_rows, 'mp', scatter_dimension=1, tiled=True)]
    dot_general x8 -> x0, matrix products: 34.6 us -> none  [the longest x3 14.3 us: contract_rows(): lax.dot_general(left, right, (((0,), (0,)), ((), ())), preferred_element_...]
    all_to_all x1 -> x0, waiting for transfers between devices: 11.5 us -> none  [local(): lax.all_to_all(summed.reshape(experts, capacity, width), 'expert', split_...]
    all_to_all x1 -> x0, starting transfers between devices: 9.54 us -> none  [local(): lax.all_to_all(summed.reshape(experts, capacity, width), 'expert', split_...]
    reshape x4 -> x0, local copies, waits for them, and re-layouts: 8.53 us -> none  [the longest x1 4.37 us: local(): jnp.stack([sent_x, sent_g], axis=1)]
  transfers between devices with their start and end apart: 4 -> 0, of which waited for: 4 -> 0; matrix products, arithmetic and copies ran while one was open for 7% -> 0% of each run, Pallas kernels for 0% -> 0%
where the time goes in v2:
time: 137 us
  Pallas kernels  132 us (96%)
  local copies, waits for them, and re-layouts  4.02 us (3%)
    pallas_call x1, Pallas kernels, local(): pl.pallas_call(functools.partial(kernel, nx, nz), name='moe_backward', ou...  132 us
    unnamed x5, local copies, waits for them, and re-layouts  4.02 us

profile of v2, /device:TPU:1, one launch (start us, length us, event | category | flops | bytes accessed | tf_op | source)
XLA Modules:
  0.0 137.4 jit_solution(13396623995641613872)
XLA Ops:
  0.6 0.7 multiply_bitcast_fusion.weight_ref
  1.3 0.0 copy-start
  1.3 0.7 copy-done
  2.0 132.0 %moe_backward.1 = (bf16[128,1024]{1,0:T(8,128)(2,1)S(1)}, bf16[8192,128]{1,0:T(8,128)(2,1)S(1)}, bf16[128,8192]{1,0:T(8,128)(2,1)S(1)}) custom-call(s32[2,128]{1,0:T(2,128)S(1)} %bitcast.9, f32[2,128]{1,0:T(2,128)S(1)} %multiply_bitcast_fusion.weight_ref, bf16[128,8192]{1,0:T(8,128)(2,1)} %act_hbm.1, bf16[128,8192]{1,0:T(8,128)(2,1)} %grad_hbm.1, ...), custom_call_target="tpu_custom_call" | custom-call | flops 5368709120 | bytes 16777216 | tf_op jit(solution)/shard_map/moe_backward/pallas_call | solution.py:317
  134.0 0.7 copy.13
  134.7 1.3 copy.14
  136.0 1.3 copy.15
Async XLA Ops:
  1.3 0.7 copy-start

commit v3 on v1

v3 whole, which is shorter than its diff:
```python
import functools
import math
import jax
import jax.numpy as jnp
from jax import lax
from jax.sharding import PartitionSpec as P
import jax.experimental.pallas as pl
import jax.experimental.pallas.tpu as pltpu

CAP = 16
NY = 4
MESH = pl.DeviceIdType.MESH
SCALE = math.sqrt(2.0 / math.pi)
CUBE = 0.044715

RINGED = 6
GROUPS = ((0, 1), (2, 3), (4,), (5,), (6, 7))
GRID = {
    32: (
        (4, 8),
        (
            ((0, 2), (1, 6), (2, 2), (3, 6)),
            ((0, 4), (1, 4), (2, 4), (3, 4)),
            ((0, 3), (1, 5), (2, 3), (3, 5)),
            ((0, 5), (1, 3), (2, 5), (3, 3)),
            ((0, 6), (1, 2), (2, 6), (3, 2)),
            ((1, 7), (2, 1), (2, 7), (3, 1)),
            ((0, 0), (1, 0), (2, 0), (3, 0)),
            ((0, 1), (0, 7), (1, 1), (3, 7)),
        ),
    ),
}


def contract_cols(left, right):
    return lax.dot_general(
        left, right, (((1,), (1,)), ((), ())), preferred_element_type=jnp.float32
    )


def product(left, right):
    return jnp.dot(left, right, preferred_element_type=jnp.float32)


def kernel(
    nx, nz, chunks,
    ids_hbm, gate_hbm, keep_hbm, act_hbm, grad_hbm, win_hbm, wout_hbm,
    tokens_out, gwin_v, gwout_v,
    ids_v, gate_v, keep_v, act_v, grad_v, sent, sent_near, rows, win_v, wout_v, win_all, hid_grad, active_v,
    back_sent, back,
    load_sem, win_send, win_recv, out_send, out_recv, ring_send, left_recv, right_recv,
    far_recv, core_recv, hid_send, hid_recv, pair_send, pair_recv, back_send, back_recv,
):
    experts = nx * nz
    toks, width = act_v.shape[1:]
    parts = 2 * NY
    total = rows.shape[2]
    span = total // len(chunks)
    count = len(chunks)
    final = GROUPS.index((RINGED - 1,))
    half = span // 2
    ff = win_v.shape[1]
    me_e = lax.axis_index("expert")
    me_m = lax.axis_index("mp")
    mx, mz = me_e // nz, lax.rem(me_e, nz)
    my, mc = me_m // 2, lax.rem(me_m, 2)

    def expert_at(dx, dz):
        return {"expert": lax.rem(mx + dx, nx) * nz + lax.rem(mz + dz, nz)}

    def up(dy):
        return lax.rem(my + dy, NY)

    right, left, far = up(1), up(NY - 1), up(2)
    other = {"mp": my * 2 + 1 - mc}

    def mate(y):
        return {"mp": y * 2 + mc}

    def column(y):
        return pl.ds(pl.multiple_of((y * 2 + mc) * width, width), width)

    small = [
        pltpu.make_async_copy(ids_hbm, ids_v, load_sem.at[2, 0]),
        pltpu.make_async_copy(gate_hbm, gate_v, load_sem.at[2, 1]),
        pltpu.make_async_copy(keep_hbm, keep_v, load_sem.at[2, 2]),
    ]
    for load in small:
        load.start()
    loads = []
    for dy in range(NY):
        y = up(dy)
        loads.append(pltpu.make_async_copy(act_hbm.at[:, column(y)], act_v.at[y], load_sem.at[0, dy]))
        loads.append(pltpu.make_async_copy(grad_hbm.at[:, column(y)], grad_v.at[y], load_sem.at[1, dy]))
    loads.append(pltpu.make_async_copy(win_hbm, win_v, load_sem.at[0, NY]))
    loads.append(pltpu.make_async_copy(wout_hbm, wout_v, load_sem.at[1, NY]))
    for load in loads:
        load.start()

    barrier = pltpu.get_barrier_semaphore()

    @pl.loop(1, experts)
    def _(step):
        pl.semaphore_signal(
            barrier, inc=1, device_id=expert_at(step // nz, lax.rem(step, nz)), device_id_type=MESH
        )

    @pl.loop(1, parts)
    def _(step):
        pl.semaphore_signal(
            barrier, inc=1, device_id={"mp": lax.rem(me_m + step, parts)}, device_id_type=MESH
        )

    for load in small:
        load.wait()
    ids = ids_v[...]
    weights = gate_v[...] * keep_v[...].astype(jnp.float32)
    lane_e = lax.broadcasted_iota(jnp.int32, (experts, toks), 0)
    chosen = [(lane_e == ids[k : k + 1, :]).astype(jnp.float32) for k in range(2)]
    before = lax.broadcasted_iota(jnp.int32, (toks, toks), 0)
    after = lax.broadcasted_iota(jnp.int32, (toks, toks), 1)
    upper = (before < after).astype(jnp.bfloat16)
    earlier = product((chosen[0] + chosen[1]).astype(jnp.bfloat16), upper)
    dx = lane_e // nz - mx
    dx = jnp.where(dx < 0, dx + nx, dx)
    dz = lane_e % nz - mz
    dz = jnp.where(dz < 0, dz + nz, dz)
    offset = dx * nz + dz
    base = jnp.zeros((experts, toks), jnp.float32)
    offsets = [pair for chunk in chunks for pair in chunk]
    for at, (ox, oz) in enumerate(offsets):
        base = jnp.where(offset == ox * nz + oz, float(at * CAP), base)
    places = [
        jnp.sum(chosen[k] * (earlier + base), axis=0, keepdims=True).astype(jnp.int32)
        for k in range(2)
    ]

    def select(start):
        lanes = lax.broadcasted_iota(jnp.int32, (span, toks), 0) + start
        hit = [lanes == places[k] for k in range(2)]
        picked = jnp.logical_or(hit[0], hit[1]).astype(jnp.float32)
        factor = jnp.where(hit[0], weights[0:1, :], 0.0) + jnp.where(hit[1], weights[1:2, :], 0.0)
        return picked, jnp.sum(factor, axis=1, keepdims=True)

    pl.semaphore_wait(barrier, experts - 1 + parts - 1)

    own = pl.ds(pl.multiple_of(me_m * width, width), width)
    pltpu.make_async_copy(win_hbm.at[own], win_all.at[me_m], win_recv).start()

    @pl.loop(1, parts)
    def _(step):
        to = lax.rem(me_m + step, parts)
        pltpu.make_async_remote_copy(
            win_hbm.at[pl.ds(pl.multiple_of(to * width, width), width)], win_all.at[me_m],
            win_send, win_recv, device_id={"mp": to}, device_id_type=MESH,
        ).start()

    def build(k):
        here = pl.ds(k * span, span)
        picked, factor = select(k * span)
        picked = picked.astype(jnp.bfloat16)
        sent[here, pl.ds(0, width)] = product(picked, act_v[my]).astype(jnp.bfloat16)
        sent[here, pl.ds(width, width)] = (factor * product(picked, grad_v[my])).astype(jnp.bfloat16)

    def launch(k):
        for at, (ox, oz) in enumerate(chunks[k]):
            here = pl.ds(k * span + at * CAP, CAP)
            pltpu.make_async_remote_copy(
                sent.at[here], rows.at[my, mc, here], out_send.at[k], out_recv.at[k],
                device_id=expert_at(ox, oz), device_id_type=MESH,
            ).start()

    def build_near(k):
        picked, factor = select(k * span)
        picked = picked.astype(jnp.bfloat16)
        for y in range(NY):
            wide = factor * product(picked, grad_v[y])
            sent_near[k - RINGED, y, :, pl.ds(0, width)] = product(picked, act_v[y]).astype(jnp.bfloat16)
            sent_near[k - RINGED, y, :, pl.ds(width, width)] = wide.astype(jnp.bfloat16)

    def launch_near(k):
        for at, (ox, oz) in enumerate(chunks[k]):
            here = pl.ds(k * span + at * CAP, CAP)
            source = sent_near.at[k - RINGED, :, pl.ds(at * CAP, CAP)]
            if (ox, oz) == (0, 0):
                pltpu.make_async_copy(source, rows.at[:, mc, here], out_recv.at[k]).start()
            else:
                pltpu.make_async_remote_copy(
                    source, rows.at[:, mc, here], out_send.at[k], out_recv.at[k],
                    device_id=expert_at(ox, oz), device_id_type=MESH,
                ).start()

    def launched(k):
        arrived(sent.at[pl.ds(k * span, span)], out_send.at[k])

    near_x, near_z = range(RINGED, count)
    loads[0].wait()
    loads[1].wait()
    build(0)
    launch(0)
    build(1)
    launch(1)
    for load in loads[2 : 2 * NY]:
        load.wait()
    build_near(near_x)
    launch_near(near_x)
    for k in range(2, RINGED):
        build(k)
    build_near(near_z)

    def launched_near(k):
        gone = span - CAP if (0, 0) in chunks[k] else span
        if gone:
            arrived(sent_near.at[k - RINGED, :, pl.ds(0, gone)], out_send.at[k])

    begun = []
    circling = []

    def push(ref, send, recv, device):
        copy = pltpu.make_async_remote_copy(
            ref, ref, send, recv, device_id=device, device_id_type=MESH
        )
        copy.start()
        begun.append(copy)
        return copy

    def arrived(ref, sem):
        pltpu.make_async_copy(ref, ref, sem).wait()

    def stage_own(k):
        ref = rows.at[my, mc, pl.ds(k * span, span)]
        arrived(ref, out_recv.at[k])
        if k > 1:
            for copy in circling[k - 2]:
                copy.wait_send()
        circling.append([
            push(ref, ring_send.at[0, k], left_recv.at[k], mate(right)),
            push(ref, ring_send.at[1, k], right_recv.at[k], mate(left)),
        ])
        if k < RINGED - 2:
            del begun[-2:]
        push(ref, ring_send.at[2, k], core_recv.at[k], other)

    def stage_side(k):
        at = k * span
        ref = rows.at[left, mc, pl.ds(at, span)]
        arrived(ref, left_recv.at[k])
        push(rows.at[left, mc, pl.ds(at, half)], ring_send.at[3, k], far_recv.at[0, k], mate(right))
        push(ref, ring_send.at[4, k], core_recv.at[k], other)
        ref = rows.at[right, mc, pl.ds(at, span)]
        arrived(ref, right_recv.at[k])
        push(rows.at[right, mc, pl.ds(at + half, half)], ring_send.at[5, k], far_recv.at[1, k], mate(left))
        push(ref, ring_send.at[6, k], core_recv.at[k], other)

    def stage_far(k):
        at = k * span
        arrived(rows.at[far, mc, pl.ds(at, half)], far_recv.at[0, k])
        arrived(rows.at[far, mc, pl.ds(at + half, half)], far_recv.at[1, k])
        push(rows.at[far, mc, pl.ds(at, span)], ring_send.at[7, k], core_recv.at[k], other)

    def stage_near(k):
        ref = rows.at[:, mc, pl.ds(k * span, span)]
        arrived(ref, out_recv.at[k])
        push(ref, ring_send.at[0, k], core_recv.at[k], other)

    def stage_hidden(k):
        at, size = GROUPS[k][0] * span, len(GROUPS[k]) * span
        for chunk in GROUPS[k]:
            arrived(rows.at[:, 0, pl.ds(chunk * span, span)], core_recv.at[chunk])

        def add(part, sums):
            hidden, grad_act = sums
            here = pl.ds(pl.multiple_of(part * width, width), width)
            block = rows[part // 2, lax.rem(part, 2), pl.ds(at, size), :]
            hidden = hidden + product(block[:, :width], win_v[here, :])
            grad_act = grad_act + contract_cols(block[:, width:], wout_v[:, here])
            return hidden, grad_act

        zero = jnp.zeros((size, ff), jnp.float32)
        hidden, grad_act = lax.fori_loop(0, parts, add, (zero, zero))
        square = hidden * hidden
        tanh = jnp.tanh(SCALE * (hidden + CUBE * (square * hidden)))
        active = 0.5 * hidden * (1.0 + tanh)
        slope = 0.5 * (1.0 + tanh) + 0.5 * hidden * (1.0 - tanh * tanh) * (
            SCALE * (1.0 + 3.0 * CUBE * square)
        )
        active_v[pl.ds(at, size), :] = active.astype(jnp.bfloat16)
        hid_grad[my, mc, pl.ds(at, size), :] = (grad_act * slope).astype(jnp.bfloat16)
        ref = hid_grad.at[my, mc, pl.ds(at, size)]
        if k == final:
            for step in range(1, parts):
                to = {"mp": lax.rem(me_m + step, parts)}
                push(ref, hid_send.at[step - 1, k], hid_recv.at[k], to)
        else:
            for side, y in enumerate((right, left, far)):
                push(ref, hid_send.at[side, k], hid_recv.at[k], mate(y))

    def stage_pair(k):
        at, size = GROUPS[k][0] * span, len(GROUPS[k]) * span
        arrived(hid_grad.at[pl.ds(0, NY - 1), 0, pl.ds(at, size)], hid_recv.at[k])
        push(hid_grad.at[:, mc, pl.ds(at, size)], pair_send.at[k], pair_recv.at[k], other)

    def stage_back(k):
        at, size = GROUPS[k][0] * span, len(GROUPS[k]) * span
        if k == final:
            arrived(hid_grad.at[0, 0, pl.ds(0, (parts - 1) * size)], hid_recv.at[k])
        else:
            arrived(hid_grad.at[:, 0, pl.ds(at, size)], pair_recv.at[k])
        grads = jnp.concatenate(
            [hid_grad[s // 2, s % 2, pl.ds(at, size), :] for s in range(parts)], axis=1
        )
        tile = min(256, width)

        @pl.loop(0, width // tile)
        def _(step):
            here = pl.ds(pl.multiple_of(step * tile, tile), tile)
            block = jnp.concatenate([win_all[s, here, :] for s in range(parts)], axis=1)
            back_sent[pl.ds(at, size), here] = contract_cols(grads, block).astype(jnp.bfloat16)

        for step, (ox, oz) in enumerate(offsets[at // CAP : (at + size) // CAP]):
            here = pl.ds(at + step * CAP, CAP)
            if (ox, oz) == (0, 0):
                pltpu.make_async_copy(back_sent.at[here], back.at[here], back_recv).start()
            else:
                pltpu.make_async_remote_copy(
                    back_sent.at[here], back.at[here], back_send, back_recv,
                    device_id=expert_at(nx - ox, nz - oz), device_id_type=MESH,
                ).start()

    tile = min(512, width)

    def grad_wout():
        active_t = active_v[...].astype(jnp.float32).T.astype(jnp.bfloat16)

        @pl.loop(0, parts)
        def _(part):
            for piece in range(0, width, tile):
                here = pl.ds(pl.multiple_of(part * width + piece, tile), tile)
                block = rows[part // 2, lax.rem(part, 2), :, pl.ds(width + piece, tile)]
                gwout_v[:, here] = product(active_t, block).astype(jnp.bfloat16)

    def grad_win():
        hid_t = hid_grad[my, mc].astype(jnp.float32).T.astype(jnp.bfloat16)

        @pl.loop(0, parts)
        def _(part):
            for piece in range(0, width, tile):
                here = pl.ds(pl.multiple_of(part * width + piece, tile), tile)
                block = rows[part // 2, lax.rem(part, 2), :, pl.ds(piece, tile)]
                gwin_v[here, :] = product(hid_t, block).T.astype(jnp.bfloat16)

    near = len(GROUPS) - 1
    launched(0)
    launch(2)
    stage_own(0)
    launched(1)
    launch(3)
    stage_own(1)
    stage_side(0)
    launched(2)
    launch(4)
    stage_near(near_x)
    stage_own(2)
    stage_side(1)
    stage_far(0)
    launched(3)
    launch(5)
    stage_own(3)
    launched(4)
    launch_near(near_z)
    stage_side(2)
    stage_far(1)
    for load in loads[2 * NY :]:
        load.wait()
    stage_hidden(0)
    stage_own(4)
    stage_side(3)
    stage_far(2)
    stage_pair(0)
    arrived(win_all, win_recv)
    stage_back(0)
    stage_own(5)
    stage_near(near_z)
    stage_side(4)
    stage_far(3)
    stage_hidden(near)
    stage_hidden(1)
    stage_side(5)
    stage_far(4)
    stage_pair(near)
    stage_pair(1)
    stage_hidden(2)
    stage_back(near)
    stage_back(1)
    stage_far(5)
    stage_pair(2)
    stage_hidden(3)
    stage_back(2)
    grad_wout()
    stage_back(3)
    grad_win()

    arrived(back, back_recv)
    sums = jnp.zeros((toks, width), jnp.float32)
    for k in range(count):
        picked, _ = select(k * span)
        sums = sums + product(picked.T.astype(jnp.bfloat16), back[pl.ds(k * span, span), :])
    tokens_out[...] = sums.astype(jnp.bfloat16)

    launched(5)
    launched_near(near_x)
    launched_near(near_z)
    arrived(win_all.at[pl.ds(0, parts - 1)], win_send)
    arrived(back_sent.at[pl.ds(0, total - CAP)], back_send)
    for copy in begun:
        copy.wait_send()


def local(grid, activations, out_grad, expert_ids, gate_probs, keep_mask, w_input, w_output):
    (nx, nz), chunks = grid
    count = len(chunks)
    parts = lax.axis_size("mp")
    toks, model = activations.shape
    width = model // parts
    ff = w_input.shape[2]
    total = nx * nz * CAP
    span = total // count
    bf16 = jnp.bfloat16
    vmem = pl.BlockSpec(memory_space=pltpu.VMEM)
    hbm = pl.BlockSpec(memory_space=pltpu.HBM)
    dma = pltpu.SemaphoreType.DMA
    tokens, gwin, gwout = pl.pallas_call(
        functools.partial(kernel, nx, nz, chunks),
        name="moe_backward",
        out_shape=(
            pltpu.VMEM((toks, width), bf16),
            pltpu.VMEM((model, ff), bf16),
            pltpu.VMEM((ff, model), bf16),
        ),
        in_specs=[hbm] * 7,
        out_specs=(vmem, vmem, vmem),
        scratch_shapes=[
            pltpu.VMEM((2, toks), jnp.int32),
            pltpu.VMEM((2, toks), jnp.float32),
            pltpu.VMEM((2, toks), jnp.int32),
            pltpu.VMEM((NY, toks, width), bf16),
            pltpu.VMEM((NY, toks, width), bf16),
            pltpu.VMEM((RINGED * span, 2 * width), bf16),
            pltpu.VMEM((count - RINGED, NY, span, 2 * width), bf16),
            pltpu.VMEM((NY, 2, total, 2 * width), bf16),
            pltpu.VMEM((model, ff), bf16),
            pltpu.VMEM((ff, model), bf16),
            pltpu.VMEM((parts, width, ff), bf16),
            pltpu.VMEM((NY, 2, total, ff), bf16),
            pltpu.VMEM((total, ff), bf16),
            pltpu.VMEM((total, width), bf16),
            pltpu.VMEM((total, width), bf16),
            dma((3, NY + 1)),
            dma(()),
            dma(()),
            dma((count,)),
            dma((count,)),
            dma((8, count)),
            dma((RINGED,)),
            dma((RINGED,)),
            dma((2, RINGED)),
            dma((count,)),
            dma((parts - 1, count)),
            dma((count,)),
            dma((count,)),
            dma((count,)),
            dma(()),
            dma(()),
        ],
        compiler_params=pltpu.CompilerParams(
            collective_id=0, has_side_effects=True, vmem_limit_bytes=50 * 2**20
        ),
        cost_estimate=pl.CostEstimate(
            flops=10 * total * model * ff, bytes_accessed=8 * model * ff * 2, transcendentals=total * ff
        ),
    )(expert_ids.T, gate_probs.T, keep_mask.T, activations, out_grad, w_input[0], w_output[0])
    return (tokens, gwin[None], gwout[None])


def solution(mesh):
    return jax.shard_map(
        functools.partial(local, GRID[mesh.shape["expert"]]),
        mesh=mesh,
        in_specs=(
            P("expert", None),
            P("expert", None),
            P("expert", None),
            P("expert", None),
            P("expert", None),
            P("expert", None, "mp"),
            P("expert", "mp", None),
        ),
        out_specs=(P("expert", "mp"), P("expert", None, "mp"), P("expert", "mp", None)),
        check_vma=False,
    )
```

time: 313 us -> 117 us (0.37); the launches traced: 309 us -> 117 us
  waiting for transfers between devices: 165 us -> 0 us
  Pallas kernels: 0 us -> 113 us
  blocking collectives: 59.1 us -> 0 us
  matrix products: 34.6 us -> 0 us
  local copies, waits for them, and re-layouts: 24.4 us -> 3.34 us
  between operations: 13.8 us -> 0.64 us
  starting transfers between devices: 9.84 us -> 0 us
    pallas_call x0 -> x1, Pallas kernels: none -> 113 us  [local(): pl.pallas_call(functools.partial(kernel, nx, nz, chunks), name='moe_backw...]
    all_gather x2 -> x0, waiting for transfers between devices: 99.3 us -> none  [the longest x1 50.6 us: local(): rows_x = lax.all_gather(recv[:, 0], 'mp', axis=1, tiled=True)]
    all_to_all x1 -> x0, blocking collectives: 59.1 us -> none  [local(): lax.all_to_all(sent, 'expert', split_axis=0, concat_axis=0, tiled=True)]
    reduce_scatter x1 -> x0, waiting for transfers between devices: 54.3 us -> none  [local(): summed = lax.psum_scatter(grad_rows, 'mp', scatter_dimension=1, tiled=True)]
    dot_general x8 -> x0, matrix products: 34.6 us -> none  [the longest x3 14.3 us: contract_rows(): lax.dot_general(left, right, (((0,), (0,)), ((), ())), preferred_element_...]
    all_to_all x1 -> x0, waiting for transfers between devices: 11.5 us -> none  [local(): lax.all_to_all(summed.reshape(experts, capacity, width), 'expert', split_...]
    all_to_all x1 -> x0, starting transfers between devices: 9.54 us -> none  [local(): lax.all_to_all(summed.reshape(experts, capacity, width), 'expert', split_...]
    reshape x4 -> x0, local copies, waits for them, and re-layouts: 8.53 us -> none  [the longest x1 4.37 us: local(): jnp.stack([sent_x, sent_g], axis=1)]
  transfers between devices with their start and end apart: 4 -> 0, of which waited for: 4 -> 0; matrix products, arithmetic and copies ran while one was open for 7% -> 0% of each run, Pallas kernels for 0% -> 0%
where the time goes in v3:
time: 117 us
  Pallas kernels  113 us (97%)
  local copies, waits for them, and re-layouts  3.34 us (3%)
    pallas_call x1, Pallas kernels, local(): pl.pallas_call(functools.partial(kernel, nx, nz, chunks), name='moe_backw...  113 us
    unnamed x3, local copies, waits for them, and re-layouts  3.34 us

profile of v3, /device:TPU:1, one launch (start us, length us, event | category | flops | bytes accessed | tf_op | source)
XLA Modules:
  0.0 117.2 jit_solution(3780875219150931705)
XLA Ops:
  0.6 113.2 %moe_backward.1 = (bf16[128,1024]{1,0:T(8,128)(2,1)S(1)}, bf16[8192,128]{1,0:T(8,128)(2,1)S(1)}, bf16[128,8192]{1,0:T(8,128)(2,1)S(1)}) custom-call(s32[2,128]{1,0:T(2,128)} %bitcast.11, f32[2,128]{1,0:T(2,128)} %bitcast.12, s32[2,128]{1,0:T(2,128)} %bitcast.13, bf16[128,8192]{1,0:T(8,128)(2,1)} %act_hbm.1, bf16[128,8192]{1,0:T(8,128)(2,1)} %grad_hbm.1, ...), custom_call_target="tpu_custom_call" | custom-call | flops 5368709120 | bytes 16777216 | tf_op jit(solution)/shard_map/moe_backward/pallas_call | solution.py:432
  113.9 0.7 copy.13
  114.6 1.3 %copy.14 = bf16[1,8192,128]{2,1,0:T(8,128)(2,1)} copy(bf16[1,8192,128]{2,1,0:T(8,128)(2,1)S(1)} %bitcast.8) | data formatting | bytes 4194304
  115.9 1.3 %copy.15 = bf16[1,128,8192]{2,1,0:T(8,128)(2,1)} copy(bf16[1,128,8192]{2,1,0:T(8,128)(2,1)S(1)} %bitcast.7) | data formatting | bytes 4194304

commit v4 on v3

--- a/solution.py
+++ b/solution.py
@@ -24,9 +24,9 @@
             ((0, 3), (1, 5), (2, 3), (3, 5)),
             ((0, 5), (1, 3), (2, 5), (3, 3)),
             ((0, 6), (1, 2), (2, 6), (3, 2)),
-            ((1, 7), (2, 1), (2, 7), (3, 1)),
+            ((0, 1), (0, 7), (1, 7), (3, 1)),
             ((0, 0), (1, 0), (2, 0), (3, 0)),
-            ((0, 1), (0, 7), (1, 1), (3, 7)),
+            ((1, 1), (2, 1), (2, 7), (3, 7)),
         ),
     ),
 }
@@ -55,10 +55,10 @@
     toks, width = act_v.shape[1:]
     parts = 2 * NY
     total = rows.shape[2]
-    span = total // len(chunks)
+    sizes = [len(chunk) * CAP for chunk in chunks]
+    starts = [sum(sizes[:k]) for k in range(len(chunks))]
     count = len(chunks)
-    final = GROUPS.index((RINGED - 1,))
-    half = span // 2
+    direct = (GROUPS.index((RINGED - 2,)), GROUPS.index((RINGED - 1,)))
     ff = win_v.shape[1]
     me_e = lax.axis_index("expert")
     me_m = lax.axis_index("mp")
@@ -79,6 +79,20 @@
 
     def column(y):
         return pl.ds(pl.multiple_of((y * 2 + mc) * width, width), width)
+
+    barrier = pltpu.get_barrier_semaphore()
+
+    @pl.loop(1, experts)
+    def _(step):
+        pl.semaphore_signal(
+            barrier, inc=1, device_id=expert_at(step // nz, lax.rem(step, nz)), device_id_type=MESH
+        )
+
+    @pl.loop(1, parts)
+    def _(step):
+        pl.semaphore_signal(
+            barrier, inc=1, device_id={"mp": lax.rem(me_m + step, parts)}, device_id_type=MESH
+        )
 
     small = [
         pltpu.make_async_copy(ids_hbm, ids_v, load_sem.at[2, 0]),
@@ -97,19 +111,18 @@
     for load in loads:
         load.start()
 
-    barrier = pltpu.get_barrier_semaphore()
-
-    @pl.loop(1, experts)
-    def _(step):
-        pl.semaphore_signal(
-            barrier, inc=1, device_id=expert_at(step // nz, lax.rem(step, nz)), device_id_type=MESH
-        )
+    pl.semaphore_wait(barrier, experts - 1 + parts - 1)
+
+    own = pl.ds(pl.multiple_of(me_m * width, width), width)
+    pltpu.make_async_copy(win_hbm.at[own], win_all.at[me_m], win_recv).start()
 
     @pl.loop(1, parts)
     def _(step):
-        pl.semaphore_signal(
-            barrier, inc=1, device_id={"mp": lax.rem(me_m + step, parts)}, device_id_type=MESH
-        )
+        to = lax.rem(me_m + step, parts)
+        pltpu.make_async_remote_copy(
+            win_hbm.at[pl.ds(pl.multiple_of(to * width, width), width)], win_all.at[me_m],
+            win_send, win_recv, device_id={"mp": to}, device_id_type=MESH,
+        ).start()
 
     for load in small:
         load.wait()
@@ -135,53 +148,42 @@
         for k in range(2)
     ]
 
-    def select(start):
-        lanes = lax.broadcasted_iota(jnp.int32, (span, toks), 0) + start
+    def select(k):
+        lanes = lax.broadcasted_iota(jnp.int32, (sizes[k], toks), 0) + starts[k]
         hit = [lanes == places[k] for k in range(2)]
         picked = jnp.logical_or(hit[0], hit[1]).astype(jnp.float32)
         factor = jnp.where(hit[0], weights[0:1, :], 0.0) + jnp.where(hit[1], weights[1:2, :], 0.0)
         return picked, jnp.sum(factor, axis=1, keepdims=True)
 
-    pl.semaphore_wait(barrier, experts - 1 + parts - 1)
-
-    own = pl.ds(pl.multiple_of(me_m * width, width), width)
-    pltpu.make_async_copy(win_hbm.at[own], win_all.at[me_m], win_recv).start()
-
-    @pl.loop(1, parts)
-    def _(step):
-        to = lax.rem(me_m + step, parts)
-        pltpu.make_async_remote_copy(
-            win_hbm.at[pl.ds(pl.multiple_of(to * width, width), width)], win_all.at[me_m],
-            win_send, win_recv, device_id={"mp": to}, device_id_type=MESH,
-        ).start()
-
     def build(k):
-        here = pl.ds(k * span, span)
-        picked, factor = select(k * span)
+        here = pl.ds(starts[k], sizes[k])
+        picked, factor = select(k)
         picked = picked.astype(jnp.bfloat16)
         sent[here, pl.ds(0, width)] = product(picked, act_v[my]).astype(jnp.bfloat16)
         sent[here, pl.ds(width, width)] = (factor * product(picked, grad_v[my])).astype(jnp.bfloat16)
 
     def launch(k):
         for at, (ox, oz) in enumerate(chunks[k]):
-            here = pl.ds(k * span + at * CAP, CAP)
+            here = pl.ds(starts[k] + at * CAP, CAP)
             pltpu.make_async_remote_copy(
                 sent.at[here], rows.at[my, mc, here], out_send.at[k], out_recv.at[k],
                 device_id=expert_at(ox, oz), device_id_type=MESH,
             ).start()
 
+    near_at = starts[RINGED]
+
     def build_near(k):
-        picked, factor = select(k * span)
+        picked, factor = select(k)
         picked = picked.astype(jnp.bfloat16)
         for y in range(NY):
             wide = factor * product(picked, grad_v[y])
-            sent_near[k - RINGED, y, :, pl.ds(0, width)] = product(picked, act_v[y]).astype(jnp.bfloat16)
-            sent_near[k - RINGED, y, :, pl.ds(width, width)] = wide.astype(jnp.bfloat16)
+            sent_near[y, pl.ds(starts[k] - near_at, sizes[k]), pl.ds(0, width)] = product(picked, act_v[y]).astype(jnp.bfloat16)
+            sent_near[y, pl.ds(starts[k] - near_at, sizes[k]), pl.ds(width, width)] = wide.astype(jnp.bfloat16)
 
     def launch_near(k):
         for at, (ox, oz) in enumerate(chunks[k]):
-            here = pl.ds(k * span + at * CAP, CAP)
-            source = sent_near.at[k - RINGED, :, pl.ds(at * CAP, CAP)]
+            here = pl.ds(starts[k] + at * CAP, CAP)
+            source = sent_near.at[:, pl.ds(starts[k] - near_at + at * CAP, CAP)]
             if (ox, oz) == (0, 0):
                 pltpu.make_async_copy(source, rows.at[:, mc, here], out_recv.at[k]).start()
             else:
@@ -191,7 +193,7 @@
                 ).start()
 
     def launched(k):
-        arrived(sent.at[pl.ds(k * span, span)], out_send.at[k])
+        arrived(sent.at[pl.ds(starts[k], sizes[k])], out_send.at[k])
 
     near_x, near_z = range(RINGED, count)
     loads[0].wait()
@@ -209,9 +211,9 @@
     build_near(near_z)
 
     def launched_near(k):
-        gone = span - CAP if (0, 0) in chunks[k] else span
+        gone = sizes[k] - CAP if (0, 0) in chunks[k] else sizes[k]
         if gone:
-            arrived(sent_near.at[k - RINGED, :, pl.ds(0, gone)], out_send.at[k])
+            arrived(sent_near.at[:, pl.ds(0, gone)], out_send.at[k])
 
     begun = []
     circling = []
@@ -228,7 +230,7 @@
         pltpu.make_async_copy(ref, ref, sem).wait()
 
     def stage_own(k):
-        ref = rows.at[my, mc, pl.ds(k * span, span)]
+        ref = rows.at[my, mc, pl.ds(starts[k], sizes[k])]
         arrived(ref, out_recv.at[k])
         if k > 1:
             for copy in circling[k - 2]:
@@ -242,42 +244,64 @@
         push(ref, ring_send.at[2, k], core_recv.at[k], other)
 
     def stage_side(k):
-        at = k * span
-        ref = rows.at[left, mc, pl.ds(at, span)]
+        at, size, half = starts[k], sizes[k], sizes[k] // 2
+        ref = rows.at[left, mc, pl.ds(at, size)]
         arrived(ref, left_recv.at[k])
         push(rows.at[left, mc, pl.ds(at, half)], ring_send.at[3, k], far_recv.at[0, k], mate(right))
         push(ref, ring_send.at[4, k], core_recv.at[k], other)
-        ref = rows.at[right, mc, pl.ds(at, span)]
+        ref = rows.at[right, mc, pl.ds(at, size)]
         arrived(ref, right_recv.at[k])
         push(rows.at[right, mc, pl.ds(at + half, half)], ring_send.at[5, k], far_recv.at[1, k], mate(left))
         push(ref, ring_send.at[6, k], core_recv.at[k], other)
 
     def stage_far(k):
-        at = k * span
+        at, size, half = starts[k], sizes[k], sizes[k] // 2
         arrived(rows.at[far, mc, pl.ds(at, half)], far_recv.at[0, k])
         arrived(rows.at[far, mc, pl.ds(at + half, half)], far_recv.at[1, k])
-        push(rows.at[far, mc, pl.ds(at, span)], ring_send.at[7, k], core_recv.at[k], other)
+        recv = core_recv.at[count if k == RINGED - 1 else k]
+        push(rows.at[far, mc, pl.ds(at, size)], ring_send.at[7, k], recv, other)
 
     def stage_near(k):
-        ref = rows.at[:, mc, pl.ds(k * span, span)]
+        ref = rows.at[:, mc, pl.ds(starts[k], sizes[k])]
         arrived(ref, out_recv.at[k])
         push(ref, ring_send.at[0, k], core_recv.at[k], other)
 
-    def stage_hidden(k):
-        at, size = GROUPS[k][0] * span, len(GROUPS[k]) * span
+    def place(k):
+        return starts[GROUPS[k][0]], sum(sizes[chunk] for chunk in GROUPS[k])
+
+    def add_part(y, core, here, sums):
+        hidden, grad_act = sums
+        part = pl.ds(pl.multiple_of((y * 2 + core) * width, width), width)
+        block = rows[y, core, here, :]
+        hidden = hidden + product(block[:, :width], win_v[part, :])
+        grad_act = grad_act + contract_cols(block[:, width:], wout_v[:, part])
+        return hidden, grad_act
+
+    def stage_sums(k):
+        at, size = place(k)
+        here = pl.ds(at, size)
+        zero = jnp.zeros((size, ff), jnp.float32)
+        sums = (zero, zero)
+        if GROUPS[k] == (RINGED - 1,):
+            arrived(rows.at[pl.ds(0, NY - 1), 0, here], core_recv.at[RINGED - 1])
+            for y in (my, left, right):
+                sums = lax.fori_loop(0, 2, lambda core, held, y=y: add_part(y, core, here, held), sums)
+            return sums
         for chunk in GROUPS[k]:
-            arrived(rows.at[:, 0, pl.ds(chunk * span, span)], core_recv.at[chunk])
-
-        def add(part, sums):
-            hidden, grad_act = sums
-            here = pl.ds(pl.multiple_of(part * width, width), width)
-            block = rows[part // 2, lax.rem(part, 2), pl.ds(at, size), :]
-            hidden = hidden + product(block[:, :width], win_v[here, :])
-            grad_act = grad_act + contract_cols(block[:, width:], wout_v[:, here])
-            return hidden, grad_act
-
-        zero = jnp.zeros((size, ff), jnp.float32)
-        hidden, grad_act = lax.fori_loop(0, parts, add, (zero, zero))
+            arrived(rows.at[:, 0, pl.ds(starts[chunk], sizes[chunk])], core_recv.at[chunk])
+        return lax.fori_loop(
+            0, parts, lambda part, held: add_part(part // 2, lax.rem(part, 2), here, held), sums
+        )
+
+    def stage_hidden(k, sums=None):
+        at, size = place(k)
+        if sums is None:
+            sums = stage_sums(k)
+        else:
+            here = pl.ds(at, size)
+            arrived(rows.at[far, 1 - mc, here], core_recv.at[count])
+            sums = lax.fori_loop(0, 2, lambda core, held: add_part(far, core, here, held), sums)
+        hidden, grad_act = sums
         square = hidden * hidden
         tanh = jnp.tanh(SCALE * (hidden + CUBE * (square * hidden)))
         active = 0.5 * hidden * (1.0 + tanh)
@@ -287,7 +311,7 @@
         active_v[pl.ds(at, size), :] = active.astype(jnp.bfloat16)
         hid_grad[my, mc, pl.ds(at, size), :] = (grad_act * slope).astype(jnp.bfloat16)
         ref = hid_grad.at[my, mc, pl.ds(at, size)]
-        if k == final:
+        if k in direct:
             for step in range(1, parts):
                 to = {"mp": lax.rem(me_m + step, parts)}
                 push(ref, hid_send.at[step - 1, k], hid_recv.at[k], to)
@@ -296,13 +320,13 @@
                 push(ref, hid_send.at[side, k], hid_recv.at[k], mate(y))
 
     def stage_pair(k):
-        at, size = GROUPS[k][0] * span, len(GROUPS[k]) * span
+        at, size = place(k)
         arrived(hid_grad.at[pl.ds(0, NY - 1), 0, pl.ds(at, size)], hid_recv.at[k])
         push(hid_grad.at[:, mc, pl.ds(at, size)], pair_send.at[k], pair_recv.at[k], other)
 
     def stage_back(k):
-        at, size = GROUPS[k][0] * span, len(GROUPS[k]) * span
-        if k == final:
+        at, size = place(k)
+        if k in direct:
             arrived(hid_grad.at[0, 0, pl.ds(0, (parts - 1) * size)], hid_recv.at[k])
         else:
             arrived(hid_grad.at[:, 0, pl.ds(at, size)], pair_recv.at[k])
@@ -320,10 +344,10 @@
         for step, (ox, oz) in enumerate(offsets[at // CAP : (at + size) // CAP]):
             here = pl.ds(at + step * CAP, CAP)
             if (ox, oz) == (0, 0):
-                pltpu.make_async_copy(back_sent.at[here], back.at[here], back_recv).start()
+                pltpu.make_async_copy(back_sent.at[here], back.at[here], back_recv.at[k]).start()
             else:
                 pltpu.make_async_remote_copy(
-                    back_sent.at[here], back.at[here], back_send, back_recv,
+                    back_sent.at[here], back.at[here], back_send, back_recv.at[k],
                     device_id=expert_at(nx - ox, nz - oz), device_id_type=MESH,
                 ).start()
 
@@ -380,31 +404,34 @@
     arrived(win_all, win_recv)
     stage_back(0)
     stage_own(5)
-    stage_near(near_z)
     stage_side(4)
     stage_far(3)
+    stage_near(near_z)
+    stage_hidden(1)
     stage_hidden(near)
-    stage_hidden(1)
     stage_side(5)
+    stage_pair(1)
     stage_far(4)
     stage_pair(near)
-    stage_pair(1)
+    stage_back(1)
     stage_hidden(2)
     stage_back(near)
-    stage_back(1)
+    part_sums = stage_sums(3)
     stage_far(5)
-    stage_pair(2)
-    stage_hidden(3)
+    stage_hidden(3, part_sums)
     stage_back(2)
     grad_wout()
     stage_back(3)
     grad_win()
 
-    arrived(back, back_recv)
     sums = jnp.zeros((toks, width), jnp.float32)
-    for k in range(count):
-        picked, _ = select(k * span)
-        sums = sums + product(picked.T.astype(jnp.bfloat16), back[pl.ds(k * span, span), :])
+    for group in sorted(range(len(GROUPS)), key=lambda k: k in direct):
+        at, size = place(group)
+        arrived(back.at[pl.ds(at, size)], back_recv.at[group])
+        for k in GROUPS[group]:
+            picked, _ = select(k)
+            mine = back[pl.ds(starts[k], sizes[k]), :]
+            sums = sums + product(picked.T.astype(jnp.bfloat16), mine)
     tokens_out[...] = sums.astype(jnp.bfloat16)
 
     launched(5)
@@ -424,7 +451,7 @@
     width = model // parts
     ff = w_input.shape[2]
     total = nx * nz * CAP
-    span = total // count
+    ringed = sum(len(chunk) for chunk in chunks[:RINGED]) * CAP
     bf16 = jnp.bfloat16
     vmem = pl.BlockSpec(memory_space=pltpu.VMEM)
     hbm = pl.BlockSpec(memory_space=pltpu.HBM)
@@ -445,8 +472,8 @@
             pltpu.VMEM((2, toks), jnp.int32),
             pltpu.VMEM((NY, toks, width), bf16),
             pltpu.VMEM((NY, toks, width), bf16),
-            pltpu.VMEM((RINGED * span, 2 * width), bf16),
-            pltpu.VMEM((count - RINGED, NY, span, 2 * width), bf16),
+            pltpu.VMEM((ringed, 2 * width), bf16),
+            pltpu.VMEM((NY, total - ringed, 2 * width), bf16),
             pltpu.VMEM((NY, 2, total, 2 * width), bf16),
             pltpu.VMEM((model, ff), bf16),
             pltpu.VMEM((ff, model), bf16),
@@ -464,13 +491,13 @@
             dma((RINGED,)),
             dma((RINGED,)),
             dma((2, RINGED)),
-            dma((count,)),
+            dma((count + 1,)),
             dma((parts - 1, count)),
             dma((count,)),
             dma((count,)),
             dma((count,)),
             dma(()),
-            dma(()),
+            dma((count,)),
         ],
         compiler_params=pltpu.CompilerParams(
             collective_id=0, has_side_effects=True, vmem_limit_bytes=50 * 2**20

time: 117 us -> 114 us (0.974)
  Pallas kernels: 113 us -> 110 us
    pallas_call x1, Pallas kernels: 113 us -> 110 us  [local(): pl.pallas_call(functools.partial(kernel, nx, nz, chunks), name='moe_backw...]
where the time goes in v4:
time: 114 us
  Pallas kernels  110 us (96%)
  local copies, waits for them, and re-layouts  3.34 us (3%)
    pallas_call x1, Pallas kernels, local(): pl.pallas_call(functools.partial(kernel, nx, nz, chunks), name='moe_backw...  110 us
    unnamed x3, local copies, waits for them, and re-layouts  3.34 us

profile of v4, /device:TPU:1, one launch (start us, length us, event | category | flops | bytes accessed | tf_op | source)
XLA Modules:
  0.0 113.6 jit_solution(1298849214565633158)
XLA Ops:
  0.6 109.7 %moe_backward.1 = (bf16[128,1024]{1,0:T(8,128)(2,1)S(1)}, bf16[8192,128]{1,0:T(8,128)(2,1)S(1)}, bf16[128,8192]{1,0:T(8,128)(2,1)S(1)}) custom-call(s32[2,128]{1,0:T(2,128)} %bitcast.11, f32[2,128]{1,0:T(2,128)} %bitcast.12, s32[2,128]{1,0:T(2,128)} %bitcast.13, bf16[128,8192]{1,0:T(8,128)(2,1)} %act_hbm.1, bf16[128,8192]{1,0:T(8,128)(2,1)} %grad_hbm.1, ...), custom_call_target="tpu_custom_call" | custom-call | flops 5368709120 | bytes 16777216 | tf_op jit(solution)/shard_map/moe_backward/pallas_call | solution.py:459
  110.3 0.7 copy.13
  111.0 1.3 %copy.14 = bf16[1,8192,128]{2,1,0:T(8,128)(2,1)} copy(bf16[1,8192,128]{2,1,0:T(8,128)(2,1)S(1)} %bitcast.8) | data formatting | bytes 4194304
  112.3 1.3 %copy.15 = bf16[1,128,8192]{2,1,0:T(8,128)(2,1)} copy(bf16[1,128,8192]{2,1,0:T(8,128)(2,1)S(1)} %bitcast.7) | data formatting | bytes 4194304

commit v5 on v4

--- a/solution.py
+++ b/solution.py
@@ -399,11 +399,11 @@
     stage_hidden(0)
     stage_own(4)
     stage_side(3)
+    stage_own(5)
     stage_far(2)
     stage_pair(0)
     arrived(win_all, win_recv)
     stage_back(0)
-    stage_own(5)
     stage_side(4)
     stage_far(3)
     stage_near(near_z)

time: 114 us -> 114 us (level)
  no operation moved by 1% of the time
where the time goes in v5:
time: 114 us
  Pallas kernels  110 us (96%)
  local copies, waits for them, and re-layouts  3.34 us (3%)
    pallas_call x1, Pallas kernels, local(): pl.pallas_call(functools.partial(kernel, nx, nz, chunks), name='moe_backw...  110 us
    unnamed x3, local copies, waits for them, and re-layouts  3.34 us

profile of v5, /device:TPU:1, one launch (start us, length us, event | category | flops | bytes accessed | tf_op | source)
XLA Modules:
  0.0 113.6 jit_solution(4063051067792293816)
XLA Ops:
  0.6 109.7 %moe_backward.1 = (bf16[128,1024]{1,0:T(8,128)(2,1)S(1)}, bf16[8192,128]{1,0:T(8,128)(2,1)S(1)}, bf16[128,8192]{1,0:T(8,128)(2,1)S(1)}) custom-call(s32[2,128]{1,0:T(2,128)} %bitcast.11, f32[2,128]{1,0:T(2,128)} %bitcast.12, s32[2,128]{1,0:T(2,128)} %bitcast.13, bf16[128,8192]{1,0:T(8,128)(2,1)} %act_hbm.1, bf16[128,8192]{1,0:T(8,128)(2,1)} %grad_hbm.1, ...), custom_call_target="tpu_custom_call" | custom-call | flops 5368709120 | bytes 16777216 | tf_op jit(solution)/shard_map/moe_backward/pallas_call | solution.py:459
  110.3 0.7 copy.13
  111.0 1.3 %copy.14 = bf16[1,8192,128]{2,1,0:T(8,128)(2,1)} copy(bf16[1,8192,128]{2,1,0:T(8,128)(2,1)S(1)} %bitcast.8) | data formatting | bytes 4194304
  112.3 1.3 %copy.15 = bf16[1,128,8192]{2,1,0:T(8,128)(2,1)} copy(bf16[1,128,8192]{2,1,0:T(8,128)(2,1)S(1)} %bitcast.7) | data formatting | bytes 4194304
